TPU v7x, 256 devices: a whole 4x4x8 slice. The times are simulated.
256 devices in a mesh: gx: 32 (over x, z), gy: 8 (over y, core).
Axes of the slice: x: 4, y: 4, z: 8, core: 2. Of those that a mesh axis runs over, the one named last changes fastest.
Arguments:
- probes: bfloat16 [64, 256, 128, 128], P(None, 'gx', 'gy'), may hold values from -6 to 6
- permeability: float32 [256, 128, 128], P('gx', 'gy'), may hold values from 0.2 to 5
- absorption: float32 [256, 128, 128], P('gx', 'gy'), may hold values from 0.3 to 3
- sensitivity: float32 [256, 128, 128], P('gx', 'gy'), may hold values from -6 to 6
- observe_weight: float32 [256, 128, 128], P('gx', 'gy'), may hold values from 1 to 10
Outputs:
- q_basis: float32 [64, 256, 128, 128], P(None, 'gx', 'gy')
- r_factor: float32 [64, 64], replicated
All inputs are finite; a program needn't handle non-finite values.
Results may differ from a plain program's by a relative error of at most 0.0003.
Values sent between devices are 32-bit elements; how exact they have to be, the bound alone decides.
A program may use at most 128 MiB of HBM per device.

v0:
```python
import jax
import jax.numpy as jnp
from jax import lax
from jax.sharding import PartitionSpec as P

SWEEPS = 4


def padded_2(shard, sides, width):
    for axis, dim in sides:
        peers, length = (lax.axis_size(axis), shard.shape[dim])
        up = [(i, (i + 1) % peers) for i in range(peers - 1)]
        down = [(j, i) for i, j in up]
        last = lax.slice_in_dim(shard, length - width, length, axis=dim)
        first = lax.slice_in_dim(shard, 0, width, axis=dim)
        before = lax.ppermute(last, axis, up)
        after = lax.ppermute(first, axis, down)
        shard = jnp.concatenate([before, shard, after], axis=dim)
    return shard


def face_terms(kpad, absorption):
    center = kpad[1:-1, 1:-1]
    x_low = 0.5 * (center + kpad[:-2, 1:-1])
    x_high = 0.5 * (center + kpad[2:, 1:-1])
    y_low = 0.5 * (center + kpad[1:-1, :-2])
    y_high = 0.5 * (center + kpad[1:-1, 2:])
    zpad = jnp.pad(center, ((0, 0), (0, 0), (1, 1)))
    z_low = 0.5 * (center + zpad[:, :, :-2])
    z_high = 0.5 * (center + zpad[:, :, 2:])
    diag = absorption + x_low + x_high + y_low + y_high + z_low + z_high
    return ((x_low, x_high, y_low, y_high, z_low, z_high), diag)


def sweep(field, padded, rhs, coefs, diag):
    x_low, x_high, y_low, y_high, z_low, z_high = coefs
    zpad = jnp.pad(field, ((0, 0), (0, 0), (0, 0), (1, 1)))
    total = x_low * padded[:, :-2, 1:-1] + x_high * padded[:, 2:, 1:-1]
    total = total + y_low * padded[:, 1:-1, :-2] + y_high * padded[:, 1:-1, 2:]
    total = total + z_low * zpad[..., :-2] + z_high * zpad[..., 2:]
    return 0.2 * field + 0.8 * (rhs + total) / diag


def single_solve(rhs, coefs, diag):
    field = 0.8 * rhs / diag
    for step in range(SWEEPS - 1):
        padded = padded_2(field, (("gx", 1), ("gy", 2)), 1)
        field = sweep(field, padded, rhs, coefs, diag)
    return field


def lower_inverse(lower):
    width = lower.shape[0]
    identity = jnp.eye(width, dtype=jnp.float32)

    def row_step(index, inverse):
        row = lax.dynamic_slice_in_dim(lower, index, 1, 0)
        pivot = lax.dynamic_slice(lower, (index, index), (1, 1))
        unit = lax.dynamic_slice_in_dim(identity, index, 1, 0)
        partial_sum = jnp.dot(
            row, inverse, precision=lax.Precision.HIGHEST, preferred_element_type=jnp.float32
        )
        new_row = (unit - partial_sum) / pivot
        return lax.dynamic_update_slice_in_dim(inverse, new_row, index, 0)

    return lax.fori_loop(0, width, row_step, jnp.zeros((width, width), jnp.float32))


def body(probes, permeability, absorption, sensitivity, observe_weight):
    count, width_x, width_y, width_z = probes.shape
    total_cells = width_x * lax.axis_size("gx") * width_y * lax.axis_size("gy") * width_z
    source = sensitivity * probes.astype(jnp.float32)
    kpad = padded_2(permeability, (("gx", 0), ("gy", 1)), 1)
    coefs, diag = face_terms(kpad, absorption)
    forward = single_solve(source, coefs, diag)
    adjoint = single_solve(observe_weight * forward, coefs, diag)
    responses = (sensitivity * adjoint).reshape(count, -1)
    gram = jnp.dot(
        responses, responses.T, precision=lax.Precision.HIGHEST, preferred_element_type=jnp.float32
    ) / float(total_cells)
    summed = lax.psum(gram, ("gx", "gy"))
    r_factor = jnp.linalg.cholesky(summed).T
    inverse = lower_inverse(r_factor.T)
    q_basis = jnp.dot(
        inverse, responses, precision=lax.Precision.HIGHEST, preferred_element_type=jnp.float32
    )
    return (q_basis.reshape(count, width_x, width_y, width_z), r_factor)


def solution(mesh):
    return jax.shard_map(
        body,
        mesh=mesh,
        in_specs=(
            P(None, "gx", "gy", None),
            P("gx", "gy", None),
            P("gx", "gy", None),
            P("gx", "gy", None),
            P("gx", "gy", None),
        ),
        out_specs=(P(None, "gx", "gy", None), P()),
        check_vma=False,
    )
```

profile of v0, /device:TPU:1, one launch (start us, length us, event | category | flops | bytes accessed | tf_op | source)
XLA Modules:
  0.0 477.7 jit_solution(5736251679478385338)
XLA Ops:
  10.3 5.0 %collective-permute-start.2 = (f32[10,1,128]{2,1,0:T(1,128)S(1)}, f32[10,1,128]{2,1,0:T(1,128)S(1)}, u32[]{:S(2)}, u32[]{:S(2)}) collective-permute-start(f32[10,1,128]{2,1,0:T(1,128)S(1)} %get-tuple-element.132), channel_id=1, source_target_pairs={{0,1},{1,2},{2,3},{3,4},{4,5},{5,6},{6,7},{8,9},{9,10},{10,11},{11... | collective-permute-start | bytes 15368 | tf_op jit(solution)/shard_map/ppermute | solution.py:16
  29.9 9.0 %collective-permute-done.4 = f32[64,1,16,128]{3,0,2,1:T(8,128)S(1)} collective-permute-done((f32[64,1,16,128]{3,0,2,1:T(8,128)S(1)}, f32[64,1,16,128]{3,0,2,1:T(8,128)S(1)}, u32[]{:S(2)}, u32[]{:S(2)}) %collective-permute-start.4) | collective-permute-done | bytes 524320 | tf_op jit(solution)/shard_map/ppermute | solution.py:16
  38.9 5.1 %collective-permute-done.5 = f32[64,1,16,128]{3,0,2,1:T(8,128)S(1)} collective-permute-done((f32[64,1,16,128]{3,0,2,1:T(8,128)S(1)}, f32[64,1,16,128]{3,0,2,1:T(8,128)S(1)}, u32[]{:S(2)}, u32[]{:S(2)}) %collective-permute-start.5) | collective-permute-done | bytes 524320 | tf_op jit(solution)/shard_map/ppermute | solution.py:17
  56.4 7.8 %fusion.10 = f32[64,8,16,128]{3,0,2,1:T(8,128)S(1)} fusion(f32[64,8,16,128]{3,0,2,1:T(8,128)S(1)} %multiply_divide_fusion.1, f32[64,10,1,128]{3,0,2,1:T(8,128)S(1)} %collective-permute-done.7, f32[64,1,16,128]{3,0,2,1:T(8,128)S(1)} %collective-permute-done.5, f32[64,1,16,128]{3,0,2,1:T(8,128)S(1)} %collective-permute-done.4, ...), kind=kLoop, calls=%fused_computation.23 | loop fusion | flops 27262976 | bytes 12713984 | tf_op jit(solution)/shard_map/add | solution.py:41
  70.5 6.0 %collective-permute-done.8 = f32[64,1,16,128]{3,0,2,1:T(8,128)S(1)} collective-permute-done((f32[64,1,16,128]{3,0,2,1:T(8,128)S(1)}, f32[64,1,16,128]{3,0,2,1:T(8,128)S(1)}, u32[]{:S(2)}, u32[]{:S(2)}) %collective-permute-start.8) | collective-permute-done | bytes 524320 | tf_op jit(solution)/shard_map/ppermute | solution.py:16
  81.0 6.2 %collective-permute-start.10 = (f32[64,10,1,128]{3,0,2,1:T(8,128)S(1)}, f32[64,10,1,128]{3,0,2,1:T(8,128)S(1)}, u32[]{:S(2)}, u32[]{:S(2)}) collective-permute-start(f32[64,10,1,128]{3,0,2,1:T(8,128)S(1)} %get-tuple-element.115), channel_id=1, source_target_pairs={{0,1},{1,2},{2,3},{3,4},{4,5},{5,6},{6,7},{8,9},{9,10},{10,11},{11... | collective-permute-start | bytes 983048 | tf_op jit(solution)/shard_map/ppermute | solution.py:16
  95.6 7.8 %fusion.18 = f32[64,8,16,128]{3,0,2,1:T(8,128)S(1)} fusion(f32[64,8,16,128]{3,0,2,1:T(8,128)S(1)} %fusion.10, f32[64,10,1,128]{3,0,2,1:T(8,128)S(1)} %collective-permute-done.11, f32[64,1,16,128]{3,0,2,1:T(8,128)S(1)} %collective-permute-done.9, f32[64,1,16,128]{3,0,2,1:T(8,128)S(1)} %collective-permute-done.8, ...), kind=kLoop, calls=%fused_computation.31 | loop fusion | flops 27262976 | bytes 12713984 | tf_op jit(solution)/shard_map/add | solution.py:41
  108.8 6.0 %collective-permute-done.12 = f32[64,1,16,128]{3,0,2,1:T(8,128)S(1)} collective-permute-done((f32[64,1,16,128]{3,0,2,1:T(8,128)S(1)}, f32[64,1,16,128]{3,0,2,1:T(8,128)S(1)}, u32[]{:S(2)}, u32[]{:S(2)}) %collective-permute-start.12) | collective-permute-done | bytes 524320 | tf_op jit(solution)/shard_map/ppermute | solution.py:16
  119.0 6.7 %collective-permute-start.14 = (f32[64,10,1,128]{3,0,2,1:T(8,128)S(1)}, f32[64,10,1,128]{3,0,2,1:T(8,128)S(1)}, u32[]{:S(2)}, u32[]{:S(2)}) collective-permute-start(f32[64,10,1,128]{3,0,2,1:T(8,128)S(1)} %get-tuple-element.113), channel_id=1, source_target_pairs={{0,1},{1,2},{2,3},{3,4},{4,5},{5,6},{6,7},{8,9},{9,10},{10,11},{11... | collective-permute-start | bytes 983048 | tf_op jit(solution)/shard_map/ppermute | solution.py:16
  134.1 7.9 %multiply_divide_fusion = (f32[64,8,16,128]{3,0,2,1:T(8,128)S(1)}, f32[64,8,16,128]{3,0,2,1:T(8,128)S(1)}) fusion(f32[8,16,128]{2,1,0:T(8,128)S(1)} %get-tuple-element.100, f32[8,16,128]{2,1,0:T(8,128)S(1)} %get-tuple-element.106, f32[64,8,16,128]{3,0,2,1:T(8,128)S(1)} %fusion.18, f32[8,16,128]{2,1,0:T(8,128)S(1)} %get-tuple-element.105, ...), kind=kLoop, calls=%fused_computation.158 | loop fusion | flops 30408704 | bytes 16973824 | tf_op jit(solution)/shard_map/div | solution.py:45
  145.5 6.0 %collective-permute-done.16 = f32[64,1,16,128]{3,0,2,1:T(8,128)S(1)} collective-permute-done((f32[64,1,16,128]{3,0,2,1:T(8,128)S(1)}, f32[64,1,16,128]{3,0,2,1:T(8,128)S(1)}, u32[]{:S(2)}, u32[]{:S(2)}) %collective-permute-start.16) | collective-permute-done | bytes 524320 | tf_op jit(solution)/shard_map/ppermute | solution.py:16
  155.7 7.3 %collective-permute-start.18 = (f32[64,10,1,128]{3,0,2,1:T(8,128)S(1)}, f32[64,10,1,128]{3,0,2,1:T(8,128)S(1)}, u32[]{:S(2)}, u32[]{:S(2)}) collective-permute-start(f32[64,10,1,128]{3,0,2,1:T(8,128)S(1)} %get-tuple-element.111), channel_id=1, source_target_pairs={{0,1},{1,2},{2,3},{3,4},{4,5},{5,6},{6,7},{8,9},{9,10},{10,11},{11... | collective-permute-start | bytes 983048 | tf_op jit(solution)/shard_map/ppermute | solution.py:16
  171.4 13.2 %fusion.34 = f32[64,8,16,128]{3,0,2,1:T(8,128)S(1)} fusion(f32[64,8,16,128]{3,0,2,1:T(8,128)S(1)} %get-tuple-element.99, f32[64,8,16,128]{3,0,2,1:T(8,128)} %copy-done.4, f32[64,10,1,128]{3,0,2,1:T(8,128)S(1)} %collective-permute-done.19, f32[64,1,16,128]{3,0,2,1:T(8,128)S(1)} %collective-permute-done.17, f32[64,1,16,128]{3,0,2,1:T(8,128)S(1)} %collective-permute-done.16, ...), kind=kLoop, calls=%fused_computation.47 | loop fusion | flops 25165824 | bytes 14745600 | tf_op jit(solution)/shard_map/add | solution.py:41
  187.3 5.9 %collective-permute-done.20 = f32[64,1,16,128]{3,0,2,1:T(8,128)S(1)} collective-permute-done((f32[64,1,16,128]{3,0,2,1:T(8,128)S(1)}, f32[64,1,16,128]{3,0,2,1:T(8,128)S(1)}, u32[]{:S(2)}, u32[]{:S(2)}) %collective-permute-start.20) | collective-permute-done | bytes 524320 | tf_op jit(solution)/shard_map/ppermute | solution.py:16
  197.4 6.9 %collective-permute-start.22 = (f32[64,10,1,128]{3,0,2,1:T(8,128)S(1)}, f32[64,10,1,128]{3,0,2,1:T(8,128)S(1)}, u32[]{:S(2)}, u32[]{:S(2)}) collective-permute-start(f32[64,10,1,128]{3,0,2,1:T(8,128)S(1)} %get-tuple-element.109), channel_id=1, source_target_pairs={{0,1},{1,2},{2,3},{3,4},{4,5},{5,6},{6,7},{8,9},{9,10},{10,11},{11... | collective-permute-start | bytes 983048 | tf_op jit(solution)/shard_map/ppermute | solution.py:16
  212.7 13.2 %fusion.42 = f32[64,8,16,128]{3,0,2,1:T(8,128)S(1)} fusion(f32[64,8,16,128]{3,0,2,1:T(8,128)S(1)} %get-tuple-element.99, f32[64,8,16,128]{3,0,2,1:T(8,128)} %copy-done.3, f32[64,10,1,128]{3,0,2,1:T(8,128)S(1)} %collective-permute-done.23, f32[64,1,16,128]{3,0,2,1:T(8,128)S(1)} %collective-permute-done.21, f32[64,1,16,128]{3,0,2,1:T(8,128)S(1)} %collective-permute-done.20, ...), kind=kLoop, calls=%fused_computation.55 | loop fusion | flops 25165824 | bytes 14745600 | tf_op jit(solution)/shard_map/add | solution.py:41
  230.8 6.0 %collective-permute-done.24 = f32[64,1,16,128]{3,0,2,1:T(8,128)S(1)} collective-permute-done((f32[64,1,16,128]{3,0,2,1:T(8,128)S(1)}, f32[64,1,16,128]{3,0,2,1:T(8,128)S(1)}, u32[]{:S(2)}, u32[]{:S(2)}) %collective-permute-start.24) | collective-permute-done | bytes 524320 | tf_op jit(solution)/shard_map/ppermute | solution.py:16
  241.0 6.0 %collective-permute-start.26 = (f32[64,10,1,128]{3,0,2,1:T(8,128)S(1)}, f32[64,10,1,128]{3,0,2,1:T(8,128)S(1)}, u32[]{:S(2)}, u32[]{:S(2)}) collective-permute-start(f32[64,10,1,128]{3,0,2,1:T(8,128)S(1)} %get-tuple-element.107), channel_id=1, source_target_pairs={{0,1},{1,2},{2,3},{3,4},{4,5},{5,6},{6,7},{8,9},{9,10},{10,11},{11... | collective-permute-start | bytes 983048 | tf_op jit(solution)/shard_map/ppermute | solution.py:16
  255.4 14.5 %fusion.97 = f32[64,8,16,128]{3,0,2,1:T(8,128)S(1)} fusion(f32[64,8,16,128]{3,0,2,1:T(8,128)} %copy-done, f32[64,8,16,128]{3,0,2,1:T(8,128)} %copy-done.2, f32[64,10,1,128]{3,0,2,1:T(8,128)S(1)} %collective-permute-done.27, f32[64,1,16,128]{3,0,2,1:T(8,128)S(1)} %collective-permute-done.25, f32[64,1,16,128]{3,0,2,1:T(8,128)S(1)} %collective-permute-done.24, ...), kind=kLoop, calls=%fused_computation.162 | loop fusion | flops 26214400 | bytes 14811136 | tf_op jit(solution)/shard_map/mul | solution.py:77
  275.3 80.6 %psum.7 = f32[64,64]{0,1:T(8,128)S(1)} all-reduce(f32[64,64]{0,1:T(8,128)S(1)} %fusion.98), channel_id=1, replica_groups=mesh['gx'=32,'gy'=8] {'gx','gy'}, use_global_device_ids=true, to_apply=%region_0.1 | all-reduce | flops 4096 | bytes 32768 | tf_op jit(solution)/shard_map/psum | solution.py:81
  356.0 5.8 %cholesky.19 = f32[64,64]{1,0:T(8,128)S(1)} custom-call(f32[64,64]{1,0:T(8,128)S(1)} %fusion.112), custom_call_target="Cholesky" | custom-call | tf_op jit(solution)/shard_map/jit(cholesky)/cholesky | solution.py:82
  363.9 6.6 %copy.29 = f32[64,8,16,128]{3,2,1,0:T(8,128)} copy(f32[64,8,16,128]{3,0,2,1:T(8,128)} %copy-done.1) | data formatting | bytes 8388608 | tf_op jit(solution)/shard_map/mul | solution.py:77
  371.2 90.6 %while.13 = (s32[]{:T(128)}, f32[64,64]{1,0:T(8,128)S(1)}, f32[64,64]{1,0:T(8,128)S(1)}, f32[64,64]{1,0:T(8,128)S(1)}, s32[]{:T(128)}, /*index=5*/s32[]{:T(128)}) while((s32[]{:T(128)}, f32[64,64]{1,0:T(8,128)S(1)}, f32[64,64]{1,0:T(8,128)S(1)}, f32[64,64]{1,0:T(8,128)S(1)}, s32[]{:T(128)}, /*index=5*/s32[]{:T(128)}) %tuple.57), condition=%wide.region_4.5_spmd, body=%wide.region_3.4_spmd.sunk | while | flops 49282 | bytes 36181 | solution.py:66
  467.1 6.0 %fusion.94 = f32[64,8,16,128]{3,0,2,1:T(8,128)S(1)} fusion(f32[8,16,128,64]{2,1,0,3:T(8,128)S(1)} %bitcast.44, f32[64,64]{1,0:T(8,128)S(1)} %get-tuple-element.81), kind=kOutput, calls=%fused_computation.156 | convolution fusion | flops 805306368 | bytes 8404992 | tf_op jit(solution)/shard_map/dot_general | solution.py:84
  (283 shorter events, 229.4 us)
Async XLA Ops:
  24.9 14.0 %collective-permute-start.4 = (f32[64,1,16,128]{3,0,2,1:T(8,128)S(1)}, f32[64,1,16,128]{3,0,2,1:T(8,128)S(1)}, u32[]{:S(2)}, u32[]{:S(2)}) collective-permute-start(f32[64,1,16,128]{3,0,2,1:T(8,128)S(1)} %get-tuple-element.129), channel_id=1, source_target_pairs={{0,8},{8,16},{16,24},{24,32},{32,40},{40,48},{48,56},{56,64},{64,7... | collective-permute-start | bytes 1572872 | tf_op jit(solution)/shard_map/ppermute | solution.py:16
  28.6 15.4 %collective-permute-start.5 = (f32[64,1,16,128]{3,0,2,1:T(8,128)S(1)}, f32[64,1,16,128]{3,0,2,1:T(8,128)S(1)}, u32[]{:S(2)}, u32[]{:S(2)}) collective-permute-start(f32[64,1,16,128]{3,0,2,1:T(8,128)S(1)} %get-tuple-element.130), channel_id=1, source_target_pairs={{8,0},{16,8},{24,16},{32,24},{40,32},{48,40},{56,48},{64,56},{72,6... | collective-permute-start | bytes 1572872 | tf_op jit(solution)/shard_map/ppermute | solution.py:17
  44.1 7.9 %collective-permute-start.6 = (f32[64,10,1,128]{3,0,2,1:T(8,128)S(1)}, f32[64,10,1,128]{3,0,2,1:T(8,128)S(1)}, u32[]{:S(2)}, u32[]{:S(2)}) collective-permute-start(f32[64,10,1,128]{3,0,2,1:T(8,128)S(1)} %get-tuple-element.117), channel_id=1, source_target_pairs={{0,1},{1,2},{2,3},{3,4},{4,5},{5,6},{6,7},{8,9},{9,10},{10,11},{11... | collective-permute-start | bytes 983048 | tf_op jit(solution)/shard_map/ppermute | solution.py:16
  48.0 8.4 %collective-permute-start.7 = (f32[64,10,1,128]{3,0,2,1:T(8,128)S(1)}, f32[64,10,1,128]{3,0,2,1:T(8,128)S(1)}, u32[]{:S(2)}, u32[]{:S(2)}) collective-permute-start(f32[64,10,1,128]{3,0,2,1:T(8,128)S(1)} %get-tuple-element.118), channel_id=1, source_target_pairs={{1,0},{2,1},{3,2},{4,3},{5,4},{6,5},{7,6},{9,8},{10,9},{11,10},{12... | collective-permute-start | bytes 983048 | tf_op jit(solution)/shard_map/ppermute | solution.py:17
  64.3 12.2 %collective-permute-start.8 = (f32[64,1,16,128]{3,0,2,1:T(8,128)S(1)}, f32[64,1,16,128]{3,0,2,1:T(8,128)S(1)}, u32[]{:S(2)}, u32[]{:S(2)}) collective-permute-start(f32[64,1,16,128]{3,0,2,1:T(8,128)S(1)} %get-tuple-element.127), channel_id=1, source_target_pairs={{0,8},{8,16},{16,24},{24,32},{32,40},{40,48},{48,56},{56,64},{64,7... | collective-permute-start | bytes 1572872 | tf_op jit(solution)/shard_map/ppermute | solution.py:16
  69.2 11.7 %collective-permute-start.9 = (f32[64,1,16,128]{3,0,2,1:T(8,128)S(1)}, f32[64,1,16,128]{3,0,2,1:T(8,128)S(1)}, u32[]{:S(2)}, u32[]{:S(2)}) collective-permute-start(f32[64,1,16,128]{3,0,2,1:T(8,128)S(1)} %get-tuple-element.128), channel_id=1, source_target_pairs={{8,0},{16,8},{24,16},{32,24},{40,32},{48,40},{56,48},{64,56},{72,6... | collective-permute-start | bytes 1572872 | tf_op jit(solution)/shard_map/ppermute | solution.py:17
  81.0 10.2 %collective-permute-start.10 = (f32[64,10,1,128]{3,0,2,1:T(8,128)S(1)}, f32[64,10,1,128]{3,0,2,1:T(8,128)S(1)}, u32[]{:S(2)}, u32[]{:S(2)}) collective-permute-start(f32[64,10,1,128]{3,0,2,1:T(8,128)S(1)} %get-tuple-element.115), channel_id=1, source_target_pairs={{0,1},{1,2},{2,3},{3,4},{4,5},{5,6},{6,7},{8,9},{9,10},{10,11},{11... | collective-permute-start | bytes 983048 | tf_op jit(solution)/shard_map/ppermute | solution.py:16
  87.2 8.4 %collective-permute-start.11 = (f32[64,10,1,128]{3,0,2,1:T(8,128)S(1)}, f32[64,10,1,128]{3,0,2,1:T(8,128)S(1)}, u32[]{:S(2)}, u32[]{:S(2)}) collective-permute-start(f32[64,10,1,128]{3,0,2,1:T(8,128)S(1)} %get-tuple-element.116), channel_id=1, source_target_pairs={{1,0},{2,1},{3,2},{4,3},{5,4},{6,5},{7,6},{9,8},{10,9},{11,10},{12... | collective-permute-start | bytes 983048 | tf_op jit(solution)/shard_map/ppermute | solution.py:17
  103.5 11.3 %collective-permute-start.12 = (f32[64,1,16,128]{3,0,2,1:T(8,128)S(1)}, f32[64,1,16,128]{3,0,2,1:T(8,128)S(1)}, u32[]{:S(2)}, u32[]{:S(2)}) collective-permute-start(f32[64,1,16,128]{3,0,2,1:T(8,128)S(1)} %get-tuple-element.125), channel_id=1, source_target_pairs={{0,8},{8,16},{16,24},{24,32},{32,40},{40,48},{48,56},{56,64},{64,7... | collective-permute-start | bytes 1572872 | tf_op jit(solution)/shard_map/ppermute | solution.py:16
  107.5 11.4 %collective-permute-start.13 = (f32[64,1,16,128]{3,0,2,1:T(8,128)S(1)}, f32[64,1,16,128]{3,0,2,1:T(8,128)S(1)}, u32[]{:S(2)}, u32[]{:S(2)}) collective-permute-start(f32[64,1,16,128]{3,0,2,1:T(8,128)S(1)} %get-tuple-element.126), channel_id=1, source_target_pairs={{8,0},{16,8},{24,16},{32,24},{40,32},{48,40},{56,48},{64,56},{72,6... | collective-permute-start | bytes 1572872 | tf_op jit(solution)/shard_map/ppermute | solution.py:17
  119.0 10.7 %collective-permute-start.14 = (f32[64,10,1,128]{3,0,2,1:T(8,128)S(1)}, f32[64,10,1,128]{3,0,2,1:T(8,128)S(1)}, u32[]{:S(2)}, u32[]{:S(2)}) collective-permute-start(f32[64,10,1,128]{3,0,2,1:T(8,128)S(1)} %get-tuple-element.113), channel_id=1, source_target_pairs={{0,1},{1,2},{2,3},{3,4},{4,5},{5,6},{6,7},{8,9},{9,10},{10,11},{11... | collective-permute-start | bytes 983048 | tf_op jit(solution)/shard_map/ppermute | solution.py:16
  125.7 8.4 %collective-permute-start.15 = (f32[64,10,1,128]{3,0,2,1:T(8,128)S(1)}, f32[64,10,1,128]{3,0,2,1:T(8,128)S(1)}, u32[]{:S(2)}, u32[]{:S(2)}) collective-permute-start(f32[64,10,1,128]{3,0,2,1:T(8,128)S(1)} %get-tuple-element.114), channel_id=1, source_target_pairs={{1,0},{2,1},{3,2},{4,3},{5,4},{6,5},{7,6},{9,8},{10,9},{11,10},{12... | collective-permute-start | bytes 983048 | tf_op jit(solution)/shard_map/ppermute | solution.py:17
  142.1 9.4 %collective-permute-start.16 = (f32[64,1,16,128]{3,0,2,1:T(8,128)S(1)}, f32[64,1,16,128]{3,0,2,1:T(8,128)S(1)}, u32[]{:S(2)}, u32[]{:S(2)}) collective-permute-start(f32[64,1,16,128]{3,0,2,1:T(8,128)S(1)} %get-tuple-element.123), channel_id=1, source_target_pairs={{0,8},{8,16},{16,24},{24,32},{32,40},{40,48},{48,56},{56,64},{64,7... | collective-permute-start | bytes 1572872 | tf_op jit(solution)/shard_map/ppermute | solution.py:16
  144.2 11.4 %collective-permute-start.17 = (f32[64,1,16,128]{3,0,2,1:T(8,128)S(1)}, f32[64,1,16,128]{3,0,2,1:T(8,128)S(1)}, u32[]{:S(2)}, u32[]{:S(2)}) collective-permute-start(f32[64,1,16,128]{3,0,2,1:T(8,128)S(1)} %get-tuple-element.124), channel_id=1, source_target_pairs={{8,0},{16,8},{24,16},{32,24},{40,32},{48,40},{56,48},{64,56},{72,6... | collective-permute-start | bytes 1572872 | tf_op jit(solution)/shard_map/ppermute | solution.py:17
  155.7 11.3 %collective-permute-start.18 = (f32[64,10,1,128]{3,0,2,1:T(8,128)S(1)}, f32[64,10,1,128]{3,0,2,1:T(8,128)S(1)}, u32[]{:S(2)}, u32[]{:S(2)}) collective-permute-start(f32[64,10,1,128]{3,0,2,1:T(8,128)S(1)} %get-tuple-element.111), channel_id=1, source_target_pairs={{0,1},{1,2},{2,3},{3,4},{4,5},{5,6},{6,7},{8,9},{9,10},{10,11},{11... | collective-permute-start | bytes 983048 | tf_op jit(solution)/shard_map/ppermute | solution.py:16
  163.0 8.4 %collective-permute-start.19 = (f32[64,10,1,128]{3,0,2,1:T(8,128)S(1)}, f32[64,10,1,128]{3,0,2,1:T(8,128)S(1)}, u32[]{:S(2)}, u32[]{:S(2)}) collective-permute-start(f32[64,10,1,128]{3,0,2,1:T(8,128)S(1)} %get-tuple-element.112), channel_id=1, source_target_pairs={{1,0},{2,1},{3,2},{4,3},{5,4},{6,5},{7,6},{9,8},{10,9},{11,10},{12... | collective-permute-start | bytes 983048 | tf_op jit(solution)/shard_map/ppermute | solution.py:17
  184.7 8.5 %collective-permute-start.20 = (f32[64,1,16,128]{3,0,2,1:T(8,128)S(1)}, f32[64,1,16,128]{3,0,2,1:T(8,128)S(1)}, u32[]{:S(2)}, u32[]{:S(2)}) collective-permute-start(f32[64,1,16,128]{3,0,2,1:T(8,128)S(1)} %get-tuple-element.121), channel_id=1, source_target_pairs={{0,8},{8,16},{16,24},{24,32},{32,40},{40,48},{48,56},{56,64},{64,7... | collective-permute-start | bytes 1572872 | tf_op jit(solution)/shard_map/ppermute | solution.py:16
  186.0 11.3 %collective-permute-start.21 = (f32[64,1,16,128]{3,0,2,1:T(8,128)S(1)}, f32[64,1,16,128]{3,0,2,1:T(8,128)S(1)}, u32[]{:S(2)}, u32[]{:S(2)}) collective-permute-start(f32[64,1,16,128]{3,0,2,1:T(8,128)S(1)} %get-tuple-element.122), channel_id=1, source_target_pairs={{8,0},{16,8},{24,16},{32,24},{40,32},{48,40},{56,48},{64,56},{72,6... | collective-permute-start | bytes 1572872 | tf_op jit(solution)/shard_map/ppermute | solution.py:17
  197.4 10.9 %collective-permute-start.22 = (f32[64,10,1,128]{3,0,2,1:T(8,128)S(1)}, f32[64,10,1,128]{3,0,2,1:T(8,128)S(1)}, u32[]{:S(2)}, u32[]{:S(2)}) collective-permute-start(f32[64,10,1,128]{3,0,2,1:T(8,128)S(1)} %get-tuple-element.109), channel_id=1, source_target_pairs={{0,1},{1,2},{2,3},{3,4},{4,5},{5,6},{6,7},{8,9},{9,10},{10,11},{11... | collective-permute-start | bytes 983048 | tf_op jit(solution)/shard_map/ppermute | solution.py:16
  204.3 8.4 %collective-permute-start.23 = (f32[64,10,1,128]{3,0,2,1:T(8,128)S(1)}, f32[64,10,1,128]{3,0,2,1:T(8,128)S(1)}, u32[]{:S(2)}, u32[]{:S(2)}) collective-permute-start(f32[64,10,1,128]{3,0,2,1:T(8,128)S(1)} %get-tuple-element.110), channel_id=1, source_target_pairs={{1,0},{2,1},{3,2},{4,3},{5,4},{6,5},{7,6},{9,8},{10,9},{11,10},{12... | collective-permute-start | bytes 983048 | tf_op jit(solution)/shard_map/ppermute | solution.py:17
  226.0 10.8 %collective-permute-start.24 = (f32[64,1,16,128]{3,0,2,1:T(8,128)S(1)}, f32[64,1,16,128]{3,0,2,1:T(8,128)S(1)}, u32[]{:S(2)}, u32[]{:S(2)}) collective-permute-start(f32[64,1,16,128]{3,0,2,1:T(8,128)S(1)} %get-tuple-element.119), channel_id=1, source_target_pairs={{0,8},{8,16},{16,24},{24,32},{32,40},{40,48},{48,56},{56,64},{64,7... | collective-permute-start | bytes 1572872 | tf_op jit(solution)/shard_map/ppermute | solution.py:16
  229.5 11.4 %collective-permute-start.25 = (f32[64,1,16,128]{3,0,2,1:T(8,128)S(1)}, f32[64,1,16,128]{3,0,2,1:T(8,128)S(1)}, u32[]{:S(2)}, u32[]{:S(2)}) collective-permute-start(f32[64,1,16,128]{3,0,2,1:T(8,128)S(1)} %get-tuple-element.120), channel_id=1, source_target_pairs={{8,0},{16,8},{24,16},{32,24},{40,32},{48,40},{56,48},{64,56},{72,6... | collective-permute-start | bytes 1572872 | tf_op jit(solution)/shard_map/ppermute | solution.py:17
  241.0 10.0 %collective-permute-start.26 = (f32[64,10,1,128]{3,0,2,1:T(8,128)S(1)}, f32[64,10,1,128]{3,0,2,1:T(8,128)S(1)}, u32[]{:S(2)}, u32[]{:S(2)}) collective-permute-start(f32[64,10,1,128]{3,0,2,1:T(8,128)S(1)} %get-tuple-element.107), channel_id=1, source_target_pairs={{0,1},{1,2},{2,3},{3,4},{4,5},{5,6},{6,7},{8,9},{9,10},{10,11},{11... | collective-permute-start | bytes 983048 | tf_op jit(solution)/shard_map/ppermute | solution.py:16
  247.0 8.4 %collective-permute-start.27 = (f32[64,10,1,128]{3,0,2,1:T(8,128)S(1)}, f32[64,10,1,128]{3,0,2,1:T(8,128)S(1)}, u32[]{:S(2)}, u32[]{:S(2)}) collective-permute-start(f32[64,10,1,128]{3,0,2,1:T(8,128)S(1)} %get-tuple-element.108), channel_id=1, source_target_pairs={{1,0},{2,1},{3,2},{4,3},{5,4},{6,5},{7,6},{9,8},{10,9},{11,10},{12... | collective-permute-start | bytes 983048 | tf_op jit(solution)/shard_map/ppermute | solution.py:17
  (12 other events, 256.8 us)
where the time goes:
time: 487 us; the launch traced here: 478 us
  waiting for transfers between devices  108 us (22%)
  starting transfers between devices  88.9 us (18%)
  blocking collectives  80.6 us (17%)
  other arithmetic  77.1 us (16%)
  local copies, waits for them, and re-layouts  60.6 us (12%)
  matrix products  59.3 us (12%)
    psum x1, blocking collectives, body(): summed = lax.psum(gram, ('gx', 'gy'))  80.6 us
    ppermute x14, starting transfers between devices, padded_2(): before = lax.ppermute(last, axis, up)  65.8 us
    ppermute x14, waiting for transfers between devices, padded_2(): after = lax.ppermute(first, axis, down)  57.8 us
    ppermute x14, waiting for transfers between devices, padded_2(): before = lax.ppermute(last, axis, up)  50.6 us
    dot_general x64, matrix products, row_step(): jnp.dot(row, inverse, precision=lax.Precision.HIGHEST, preferred_element_...  50 us
    add x4, other arithmetic, sweep(): return 0.2 * field + 0.8 * (rhs + total) / diag  42 us
    dynamic_slice x64, local copies, waits for them, and re-layouts, row_step(): pivot = lax.dynamic_slice(lower, (index, index), (1, 1))  37.6 us
    ppermute x14, starting transfers between devices, padded_2(): after = lax.ppermute(first, axis, down)  23.1 us
  transfers between devices with their start and end apart: 28, of which 26 were waited for; matrix products, arithmetic and copies ran while one was open for 0% of the time, Pallas kernels for 0%

commit v1 on v0

--- a/solution.py
+++ b/solution.py
@@ -78,7 +78,7 @@
     gram = jnp.dot(
         responses, responses.T, precision=lax.Precision.HIGHEST, preferred_element_type=jnp.float32
     ) / float(total_cells)
-    summed = lax.psum(gram, ("gx", "gy"))
+    summed = lax.psum(lax.psum(gram, "gy"), "gx")
     r_factor = jnp.linalg.cholesky(summed).T
     inverse = lower_inverse(r_factor.T)
     q_basis = jnp.dot(

time: 487 us -> 566 us (1.16)
  the two profiles are of different devices: /device:TPU:1 before, /device:TPU:0 now
where the time goes in v1:
time: 566 us; the launch traced here: 557 us
  blocking collectives  168 us (30%)
  waiting for transfers between devices  113 us (20%)
  other arithmetic  77 us (14%)
  starting transfers between devices  76.4 us (13%)
  local copies, waits for them, and re-layouts  60.6 us (11%)
  matrix products  59.3 us (10%)
    psum x2, blocking collectives, body(): summed = lax.psum(lax.psum(gram, 'gy'), 'gx')  168 us
    ppermute x14, waiting for transfers between devices, padded_2(): after = lax.ppermute(first, axis, down)  70.9 us
    ppermute x14, starting transfers between devices, padded_2(): before = lax.ppermute(last, axis, up)  57.6 us
    dot_general x64, matrix products, row_step(): jnp.dot(row, inverse, precision=lax.Precision.HIGHEST, preferred_element_...  50 us
    ppermute x14, waiting for transfers between devices, padded_2(): before = lax.ppermute(last, axis, up)  42 us
    add x4, other arithmetic, sweep(): return 0.2 * field + 0.8 * (rhs + total) / diag  41.9 us
    dynamic_slice x64, local copies, waits for them, and re-layouts, row_step(): pivot = lax.dynamic_slice(lower, (index, index), (1, 1))  37.6 us
    ppermute x14, starting transfers between devices, padded_2(): after = lax.ppermute(first, axis, down)  18.7 us
  transfers between devices with their start and end apart: 28, of which 20 were waited for; matrix products, arithmetic and copies ran while one was open for 0% of the time, Pallas kernels for 0%

profile of v1, /device:TPU:0, one launch (start us, length us, event | category | flops | bytes accessed | tf_op | source)
XLA Modules:
  0.0 557.3 jit_solution(10749071057840535530)
XLA Ops:
  25.1 9.5 %collective-permute-done.4 = f32[64,1,16,128]{3,0,2,1:T(8,128)S(1)} collective-permute-done((f32[64,1,16,128]{3,0,2,1:T(8,128)S(1)}, f32[64,1,16,128]{3,0,2,1:T(8,128)S(1)}, u32[]{:S(2)}, u32[]{:S(2)}) %collective-permute-start.4) | collective-permute-done | bytes 524320 | tf_op jit(solution)/shard_map/ppermute | solution.py:16
  48.3 7.8 %fusion.10 = f32[64,8,16,128]{3,0,2,1:T(8,128)S(1)} fusion(f32[64,8,16,128]{3,0,2,1:T(8,128)S(1)} %multiply_divide_fusion.1, f32[64,10,1,128]{3,0,2,1:T(8,128)S(1)} %collective-permute-done.7, f32[64,1,16,128]{3,0,2,1:T(8,128)S(1)} %collective-permute-done.5, f32[64,1,16,128]{3,0,2,1:T(8,128)S(1)} %collective-permute-done.4, ...), kind=kLoop, calls=%fused_computation.23 | loop fusion | flops 27262976 | bytes 12713984 | tf_op jit(solution)/shard_map/add | solution.py:41
  62.7 6.5 %collective-permute-done.8 = f32[64,1,16,128]{3,0,2,1:T(8,128)S(1)} collective-permute-done((f32[64,1,16,128]{3,0,2,1:T(8,128)S(1)}, f32[64,1,16,128]{3,0,2,1:T(8,128)S(1)}, u32[]{:S(2)}, u32[]{:S(2)}) %collective-permute-start.8) | collective-permute-done | bytes 524320 | tf_op jit(solution)/shard_map/ppermute | solution.py:16
  74.0 6.2 %collective-permute-start.10 = (f32[64,10,1,128]{3,0,2,1:T(8,128)S(1)}, f32[64,10,1,128]{3,0,2,1:T(8,128)S(1)}, u32[]{:S(2)}, u32[]{:S(2)}) collective-permute-start(f32[64,10,1,128]{3,0,2,1:T(8,128)S(1)} %get-tuple-element.115), channel_id=1, source_target_pairs={{0,1},{1,2},{2,3},{3,4},{4,5},{5,6},{6,7},{8,9},{9,10},{10,11},{11... | collective-permute-start | bytes 983048 | tf_op jit(solution)/shard_map/ppermute | solution.py:16
  81.5 6.0 %collective-permute-done.11 = f32[64,10,1,128]{3,0,2,1:T(8,128)S(1)} collective-permute-done((f32[64,10,1,128]{3,0,2,1:T(8,128)S(1)}, f32[64,10,1,128]{3,0,2,1:T(8,128)S(1)}, u32[]{:S(2)}, u32[]{:S(2)}) %collective-permute-start.11) | collective-permute-done | bytes 327712 | tf_op jit(solution)/shard_map/ppermute | solution.py:17
  87.5 7.8 %fusion.18 = f32[64,8,16,128]{3,0,2,1:T(8,128)S(1)} fusion(f32[64,8,16,128]{3,0,2,1:T(8,128)S(1)} %fusion.10, f32[64,10,1,128]{3,0,2,1:T(8,128)S(1)} %collective-permute-done.11, f32[64,1,16,128]{3,0,2,1:T(8,128)S(1)} %collective-permute-done.9, f32[64,1,16,128]{3,0,2,1:T(8,128)S(1)} %collective-permute-done.8, ...), kind=kLoop, calls=%fused_computation.31 | loop fusion | flops 27262976 | bytes 12713984 | tf_op jit(solution)/shard_map/add | solution.py:41
  101.0 6.5 %collective-permute-done.12 = f32[64,1,16,128]{3,0,2,1:T(8,128)S(1)} collective-permute-done((f32[64,1,16,128]{3,0,2,1:T(8,128)S(1)}, f32[64,1,16,128]{3,0,2,1:T(8,128)S(1)}, u32[]{:S(2)}, u32[]{:S(2)}) %collective-permute-start.12) | collective-permute-done | bytes 524320 | tf_op jit(solution)/shard_map/ppermute | solution.py:16
  119.5 6.5 %collective-permute-done.15 = f32[64,10,1,128]{3,0,2,1:T(8,128)S(1)} collective-permute-done((f32[64,10,1,128]{3,0,2,1:T(8,128)S(1)}, f32[64,10,1,128]{3,0,2,1:T(8,128)S(1)}, u32[]{:S(2)}, u32[]{:S(2)}) %collective-permute-start.15) | collective-permute-done | bytes 327712 | tf_op jit(solution)/shard_map/ppermute | solution.py:17
  126.0 7.9 %multiply_divide_fusion = (f32[64,8,16,128]{3,0,2,1:T(8,128)S(1)}, f32[64,8,16,128]{3,0,2,1:T(8,128)S(1)}) fusion(f32[8,16,128]{2,1,0:T(8,128)S(1)} %get-tuple-element.100, f32[8,16,128]{2,1,0:T(8,128)S(1)} %get-tuple-element.106, f32[64,8,16,128]{3,0,2,1:T(8,128)S(1)} %fusion.18, f32[8,16,128]{2,1,0:T(8,128)S(1)} %get-tuple-element.105, ...), kind=kLoop, calls=%fused_computation.158 | loop fusion | flops 30408704 | bytes 16973824 | tf_op jit(solution)/shard_map/div | solution.py:45
  137.7 6.5 %collective-permute-done.16 = f32[64,1,16,128]{3,0,2,1:T(8,128)S(1)} collective-permute-done((f32[64,1,16,128]{3,0,2,1:T(8,128)S(1)}, f32[64,1,16,128]{3,0,2,1:T(8,128)S(1)}, u32[]{:S(2)}, u32[]{:S(2)}) %collective-permute-start.16) | collective-permute-done | bytes 524320 | tf_op jit(solution)/shard_map/ppermute | solution.py:16
  149.0 5.9 %collective-permute-start.18 = (f32[64,10,1,128]{3,0,2,1:T(8,128)S(1)}, f32[64,10,1,128]{3,0,2,1:T(8,128)S(1)}, u32[]{:S(2)}, u32[]{:S(2)}) collective-permute-start(f32[64,10,1,128]{3,0,2,1:T(8,128)S(1)} %get-tuple-element.111), channel_id=1, source_target_pairs={{0,1},{1,2},{2,3},{3,4},{4,5},{5,6},{6,7},{8,9},{9,10},{10,11},{11... | collective-permute-start | bytes 983048 | tf_op jit(solution)/shard_map/ppermute | solution.py:16
  156.7 6.6 %collective-permute-done.19 = f32[64,10,1,128]{3,0,2,1:T(8,128)S(1)} collective-permute-done((f32[64,10,1,128]{3,0,2,1:T(8,128)S(1)}, f32[64,10,1,128]{3,0,2,1:T(8,128)S(1)}, u32[]{:S(2)}, u32[]{:S(2)}) %collective-permute-start.19) | collective-permute-done | bytes 327712 | tf_op jit(solution)/shard_map/ppermute | solution.py:17
  163.3 13.1 %fusion.34 = f32[64,8,16,128]{3,0,2,1:T(8,128)S(1)} fusion(f32[64,8,16,128]{3,0,2,1:T(8,128)S(1)} %get-tuple-element.99, f32[64,8,16,128]{3,0,2,1:T(8,128)} %copy-done.4, f32[64,10,1,128]{3,0,2,1:T(8,128)S(1)} %collective-permute-done.19, f32[64,1,16,128]{3,0,2,1:T(8,128)S(1)} %collective-permute-done.17, f32[64,1,16,128]{3,0,2,1:T(8,128)S(1)} %collective-permute-done.16, ...), kind=kLoop, calls=%fused_computation.47 | loop fusion | flops 25165824 | bytes 14745600 | tf_op jit(solution)/shard_map/add | solution.py:41
  179.3 6.4 %collective-permute-done.20 = f32[64,1,16,128]{3,0,2,1:T(8,128)S(1)} collective-permute-done((f32[64,1,16,128]{3,0,2,1:T(8,128)S(1)}, f32[64,1,16,128]{3,0,2,1:T(8,128)S(1)}, u32[]{:S(2)}, u32[]{:S(2)}) %collective-permute-start.20) | collective-permute-done | bytes 524320 | tf_op jit(solution)/shard_map/ppermute | solution.py:16
  190.5 6.0 %collective-permute-start.22 = (f32[64,10,1,128]{3,0,2,1:T(8,128)S(1)}, f32[64,10,1,128]{3,0,2,1:T(8,128)S(1)}, u32[]{:S(2)}, u32[]{:S(2)}) collective-permute-start(f32[64,10,1,128]{3,0,2,1:T(8,128)S(1)} %get-tuple-element.109), channel_id=1, source_target_pairs={{0,1},{1,2},{2,3},{3,4},{4,5},{5,6},{6,7},{8,9},{9,10},{10,11},{11... | collective-permute-start | bytes 983048 | tf_op jit(solution)/shard_map/ppermute | solution.py:16
  197.9 6.7 %collective-permute-done.23 = f32[64,10,1,128]{3,0,2,1:T(8,128)S(1)} collective-permute-done((f32[64,10,1,128]{3,0,2,1:T(8,128)S(1)}, f32[64,10,1,128]{3,0,2,1:T(8,128)S(1)}, u32[]{:S(2)}, u32[]{:S(2)}) %collective-permute-start.23) | collective-permute-done | bytes 327712 | tf_op jit(solution)/shard_map/ppermute | solution.py:17
  204.6 13.1 %fusion.42 = f32[64,8,16,128]{3,0,2,1:T(8,128)S(1)} fusion(f32[64,8,16,128]{3,0,2,1:T(8,128)S(1)} %get-tuple-element.99, f32[64,8,16,128]{3,0,2,1:T(8,128)} %copy-done.3, f32[64,10,1,128]{3,0,2,1:T(8,128)S(1)} %collective-permute-done.23, f32[64,1,16,128]{3,0,2,1:T(8,128)S(1)} %collective-permute-done.21, f32[64,1,16,128]{3,0,2,1:T(8,128)S(1)} %collective-permute-done.20, ...), kind=kLoop, calls=%fused_computation.55 | loop fusion | flops 25165824 | bytes 14745600 | tf_op jit(solution)/shard_map/add | solution.py:41
  222.9 6.5 %collective-permute-done.24 = f32[64,1,16,128]{3,0,2,1:T(8,128)S(1)} collective-permute-done((f32[64,1,16,128]{3,0,2,1:T(8,128)S(1)}, f32[64,1,16,128]{3,0,2,1:T(8,128)S(1)}, u32[]{:S(2)}, u32[]{:S(2)}) %collective-permute-start.24) | collective-permute-done | bytes 524320 | tf_op jit(solution)/shard_map/ppermute | solution.py:16
  247.2 14.5 %fusion.97 = f32[64,8,16,128]{3,0,2,1:T(8,128)S(1)} fusion(f32[64,8,16,128]{3,0,2,1:T(8,128)} %copy-done, f32[64,8,16,128]{3,0,2,1:T(8,128)} %copy-done.2, f32[64,10,1,128]{3,0,2,1:T(8,128)S(1)} %collective-permute-done.27, f32[64,1,16,128]{3,0,2,1:T(8,128)S(1)} %collective-permute-done.25, f32[64,1,16,128]{3,0,2,1:T(8,128)S(1)} %collective-permute-done.24, ...), kind=kLoop, calls=%fused_computation.162 | loop fusion | flops 26214400 | bytes 14811136 | tf_op jit(solution)/shard_map/mul | solution.py:77
  267.1 28.8 %psum.14 = f32[64,64]{0,1:T(8,128)S(1)} all-reduce(f32[64,64]{0,1:T(8,128)S(1)} %fusion.98), channel_id=1, replica_groups=mesh['gx'=32,'gy'=8] {'gy'}, use_global_device_ids=true, to_apply=%region_0.1 | all-reduce | flops 4096 | bytes 32768 | tf_op jit(solution)/shard_map/psum | solution.py:81
  295.9 139.6 %psum.15 = f32[64,64]{0,1:T(8,128)S(1)} all-reduce(f32[64,64]{0,1:T(8,128)S(1)} %psum.14), channel_id=1, replica_groups=mesh['gx'=32,'gy'=8] {'gx'}, use_global_device_ids=true, to_apply=%region_1.2 | all-reduce | flops 4096 | bytes 32768 | tf_op jit(solution)/shard_map/psum | solution.py:81
  443.5 6.6 %copy.29 = f32[64,8,16,128]{3,2,1,0:T(8,128)} copy(f32[64,8,16,128]{3,0,2,1:T(8,128)} %copy-done.1) | data formatting | bytes 8388608 | tf_op jit(solution)/shard_map/mul | solution.py:77
  450.8 90.6 %while.13 = (s32[]{:T(128)}, f32[64,64]{1,0:T(8,128)S(1)}, f32[64,64]{1,0:T(8,128)S(1)}, f32[64,64]{1,0:T(8,128)S(1)}, s32[]{:T(128)}, /*index=5*/s32[]{:T(128)}) while((s32[]{:T(128)}, f32[64,64]{1,0:T(8,128)S(1)}, f32[64,64]{1,0:T(8,128)S(1)}, f32[64,64]{1,0:T(8,128)S(1)}, s32[]{:T(128)}, /*index=5*/s32[]{:T(128)}) %tuple.57), condition=%wide.region_5.6_spmd, body=%wide.region_4.5_spmd.sunk | while | flops 49282 | bytes 36181 | solution.py:66
  546.7 6.0 %fusion.94 = f32[64,8,16,128]{3,0,2,1:T(8,128)S(1)} fusion(f32[8,16,128,64]{2,1,0,3:T(8,128)S(1)} %bitcast.44, f32[64,64]{1,0:T(8,128)S(1)} %get-tuple-element.81), kind=kOutput, calls=%fused_computation.156 | convolution fusion | flops 805306368 | bytes 8404992 | tf_op jit(solution)/shard_map/dot_general | solution.py:84
  (284 shorter events, 223.4 us)
Async XLA Ops:
  3.4 5.5 collective-permute-start.1
  19.8 14.8 %collective-permute-start.4 = (f32[64,1,16,128]{3,0,2,1:T(8,128)S(1)}, f32[64,1,16,128]{3,0,2,1:T(8,128)S(1)}, u32[]{:S(2)}, u32[]{:S(2)}) collective-permute-start(f32[64,1,16,128]{3,0,2,1:T(8,128)S(1)} %get-tuple-element.129), channel_id=1, source_target_pairs={{0,8},{8,16},{16,24},{24,32},{32,40},{40,48},{48,56},{56,64},{64,7... | collective-permute-start | bytes 1572872 | tf_op jit(solution)/shard_map/ppermute | solution.py:16
  23.8 16.2 %collective-permute-start.5 = (f32[64,1,16,128]{3,0,2,1:T(8,128)S(1)}, f32[64,1,16,128]{3,0,2,1:T(8,128)S(1)}, u32[]{:S(2)}, u32[]{:S(2)}) collective-permute-start(f32[64,1,16,128]{3,0,2,1:T(8,128)S(1)} %get-tuple-element.130), channel_id=1, source_target_pairs={{8,0},{16,8},{24,16},{32,24},{40,32},{48,40},{56,48},{64,56},{72,6... | collective-permute-start | bytes 1572872 | tf_op jit(solution)/shard_map/ppermute | solution.py:17
  43.3 5.0 collective-permute-start.7
  56.2 13.0 %collective-permute-start.8 = (f32[64,1,16,128]{3,0,2,1:T(8,128)S(1)}, f32[64,1,16,128]{3,0,2,1:T(8,128)S(1)}, u32[]{:S(2)}, u32[]{:S(2)}) collective-permute-start(f32[64,1,16,128]{3,0,2,1:T(8,128)S(1)} %get-tuple-element.127), channel_id=1, source_target_pairs={{0,8},{8,16},{16,24},{24,32},{32,40},{40,48},{48,56},{56,64},{64,7... | collective-permute-start | bytes 1572872 | tf_op jit(solution)/shard_map/ppermute | solution.py:16
  61.4 12.5 %collective-permute-start.9 = (f32[64,1,16,128]{3,0,2,1:T(8,128)S(1)}, f32[64,1,16,128]{3,0,2,1:T(8,128)S(1)}, u32[]{:S(2)}, u32[]{:S(2)}) collective-permute-start(f32[64,1,16,128]{3,0,2,1:T(8,128)S(1)} %get-tuple-element.128), channel_id=1, source_target_pairs={{8,0},{16,8},{24,16},{32,24},{40,32},{48,40},{56,48},{64,56},{72,6... | collective-permute-start | bytes 1572872 | tf_op jit(solution)/shard_map/ppermute | solution.py:17
  74.0 7.5 %collective-permute-start.10 = (f32[64,10,1,128]{3,0,2,1:T(8,128)S(1)}, f32[64,10,1,128]{3,0,2,1:T(8,128)S(1)}, u32[]{:S(2)}, u32[]{:S(2)}) collective-permute-start(f32[64,10,1,128]{3,0,2,1:T(8,128)S(1)} %get-tuple-element.115), channel_id=1, source_target_pairs={{0,1},{1,2},{2,3},{3,4},{4,5},{5,6},{6,7},{8,9},{9,10},{10,11},{11... | collective-permute-start | bytes 983048 | tf_op jit(solution)/shard_map/ppermute | solution.py:16
  80.2 7.3 %collective-permute-start.11 = (f32[64,10,1,128]{3,0,2,1:T(8,128)S(1)}, f32[64,10,1,128]{3,0,2,1:T(8,128)S(1)}, u32[]{:S(2)}, u32[]{:S(2)}) collective-permute-start(f32[64,10,1,128]{3,0,2,1:T(8,128)S(1)} %get-tuple-element.116), channel_id=1, source_target_pairs={{1,0},{2,1},{3,2},{4,3},{5,4},{6,5},{7,6},{9,8},{10,9},{11,10},{12... | collective-permute-start | bytes 983048 | tf_op jit(solution)/shard_map/ppermute | solution.py:17
  95.4 12.1 %collective-permute-start.12 = (f32[64,1,16,128]{3,0,2,1:T(8,128)S(1)}, f32[64,1,16,128]{3,0,2,1:T(8,128)S(1)}, u32[]{:S(2)}, u32[]{:S(2)}) collective-permute-start(f32[64,1,16,128]{3,0,2,1:T(8,128)S(1)} %get-tuple-element.125), channel_id=1, source_target_pairs={{0,8},{8,16},{16,24},{24,32},{32,40},{40,48},{48,56},{56,64},{64,7... | collective-permute-start | bytes 1572872 | tf_op jit(solution)/shard_map/ppermute | solution.py:16
  99.7 12.5 %collective-permute-start.13 = (f32[64,1,16,128]{3,0,2,1:T(8,128)S(1)}, f32[64,1,16,128]{3,0,2,1:T(8,128)S(1)}, u32[]{:S(2)}, u32[]{:S(2)}) collective-permute-start(f32[64,1,16,128]{3,0,2,1:T(8,128)S(1)} %get-tuple-element.126), channel_id=1, source_target_pairs={{8,0},{16,8},{24,16},{32,24},{40,32},{48,40},{56,48},{64,56},{72,6... | collective-permute-start | bytes 1572872 | tf_op jit(solution)/shard_map/ppermute | solution.py:17
  112.2 7.2 %collective-permute-start.14 = (f32[64,10,1,128]{3,0,2,1:T(8,128)S(1)}, f32[64,10,1,128]{3,0,2,1:T(8,128)S(1)}, u32[]{:S(2)}, u32[]{:S(2)}) collective-permute-start(f32[64,10,1,128]{3,0,2,1:T(8,128)S(1)} %get-tuple-element.113), channel_id=1, source_target_pairs={{0,1},{1,2},{2,3},{3,4},{4,5},{5,6},{6,7},{8,9},{9,10},{10,11},{11... | collective-permute-start | bytes 983048 | tf_op jit(solution)/shard_map/ppermute | solution.py:16
  118.2 7.8 %collective-permute-start.15 = (f32[64,10,1,128]{3,0,2,1:T(8,128)S(1)}, f32[64,10,1,128]{3,0,2,1:T(8,128)S(1)}, u32[]{:S(2)}, u32[]{:S(2)}) collective-permute-start(f32[64,10,1,128]{3,0,2,1:T(8,128)S(1)} %get-tuple-element.114), channel_id=1, source_target_pairs={{1,0},{2,1},{3,2},{4,3},{5,4},{6,5},{7,6},{9,8},{10,9},{11,10},{12... | collective-permute-start | bytes 983048 | tf_op jit(solution)/shard_map/ppermute | solution.py:17
  134.0 10.2 %collective-permute-start.16 = (f32[64,1,16,128]{3,0,2,1:T(8,128)S(1)}, f32[64,1,16,128]{3,0,2,1:T(8,128)S(1)}, u32[]{:S(2)}, u32[]{:S(2)}) collective-permute-start(f32[64,1,16,128]{3,0,2,1:T(8,128)S(1)} %get-tuple-element.123), channel_id=1, source_target_pairs={{0,8},{8,16},{16,24},{24,32},{32,40},{40,48},{48,56},{56,64},{64,7... | collective-permute-start | bytes 1572872 | tf_op jit(solution)/shard_map/ppermute | solution.py:16
  136.4 12.5 %collective-permute-start.17 = (f32[64,1,16,128]{3,0,2,1:T(8,128)S(1)}, f32[64,1,16,128]{3,0,2,1:T(8,128)S(1)}, u32[]{:S(2)}, u32[]{:S(2)}) collective-permute-start(f32[64,1,16,128]{3,0,2,1:T(8,128)S(1)} %get-tuple-element.124), channel_id=1, source_target_pairs={{8,0},{16,8},{24,16},{32,24},{40,32},{48,40},{56,48},{64,56},{72,6... | collective-permute-start | bytes 1572872 | tf_op jit(solution)/shard_map/ppermute | solution.py:17
  149.0 7.7 %collective-permute-start.18 = (f32[64,10,1,128]{3,0,2,1:T(8,128)S(1)}, f32[64,10,1,128]{3,0,2,1:T(8,128)S(1)}, u32[]{:S(2)}, u32[]{:S(2)}) collective-permute-start(f32[64,10,1,128]{3,0,2,1:T(8,128)S(1)} %get-tuple-element.111), channel_id=1, source_target_pairs={{0,1},{1,2},{2,3},{3,4},{4,5},{5,6},{6,7},{8,9},{9,10},{10,11},{11... | collective-permute-start | bytes 983048 | tf_op jit(solution)/shard_map/ppermute | solution.py:16
  154.9 8.4 %collective-permute-start.19 = (f32[64,10,1,128]{3,0,2,1:T(8,128)S(1)}, f32[64,10,1,128]{3,0,2,1:T(8,128)S(1)}, u32[]{:S(2)}, u32[]{:S(2)}) collective-permute-start(f32[64,10,1,128]{3,0,2,1:T(8,128)S(1)} %get-tuple-element.112), channel_id=1, source_target_pairs={{1,0},{2,1},{3,2},{4,3},{5,4},{6,5},{7,6},{9,8},{10,9},{11,10},{12... | collective-permute-start | bytes 983048 | tf_op jit(solution)/shard_map/ppermute | solution.py:17
  176.5 9.2 %collective-permute-start.20 = (f32[64,1,16,128]{3,0,2,1:T(8,128)S(1)}, f32[64,1,16,128]{3,0,2,1:T(8,128)S(1)}, u32[]{:S(2)}, u32[]{:S(2)}) collective-permute-start(f32[64,1,16,128]{3,0,2,1:T(8,128)S(1)} %get-tuple-element.121), channel_id=1, source_target_pairs={{0,8},{8,16},{16,24},{24,32},{32,40},{40,48},{48,56},{56,64},{64,7... | collective-permute-start | bytes 1572872 | tf_op jit(solution)/shard_map/ppermute | solution.py:16
  178.0 12.4 %collective-permute-start.21 = (f32[64,1,16,128]{3,0,2,1:T(8,128)S(1)}, f32[64,1,16,128]{3,0,2,1:T(8,128)S(1)}, u32[]{:S(2)}, u32[]{:S(2)}) collective-permute-start(f32[64,1,16,128]{3,0,2,1:T(8,128)S(1)} %get-tuple-element.122), channel_id=1, source_target_pairs={{8,0},{16,8},{24,16},{32,24},{40,32},{48,40},{56,48},{64,56},{72,6... | collective-permute-start | bytes 1572872 | tf_op jit(solution)/shard_map/ppermute | solution.py:17
  190.5 7.4 %collective-permute-start.22 = (f32[64,10,1,128]{3,0,2,1:T(8,128)S(1)}, f32[64,10,1,128]{3,0,2,1:T(8,128)S(1)}, u32[]{:S(2)}, u32[]{:S(2)}) collective-permute-start(f32[64,10,1,128]{3,0,2,1:T(8,128)S(1)} %get-tuple-element.109), channel_id=1, source_target_pairs={{0,1},{1,2},{2,3},{3,4},{4,5},{5,6},{6,7},{8,9},{9,10},{10,11},{11... | collective-permute-start | bytes 983048 | tf_op jit(solution)/shard_map/ppermute | solution.py:16
  196.6 8.0 %collective-permute-start.23 = (f32[64,10,1,128]{3,0,2,1:T(8,128)S(1)}, f32[64,10,1,128]{3,0,2,1:T(8,128)S(1)}, u32[]{:S(2)}, u32[]{:S(2)}) collective-permute-start(f32[64,10,1,128]{3,0,2,1:T(8,128)S(1)} %get-tuple-element.110), channel_id=1, source_target_pairs={{1,0},{2,1},{3,2},{4,3},{5,4},{6,5},{7,6},{9,8},{10,9},{11,10},{12... | collective-permute-start | bytes 983048 | tf_op jit(solution)/shard_map/ppermute | solution.py:17
  217.8 11.6 %collective-permute-start.24 = (f32[64,1,16,128]{3,0,2,1:T(8,128)S(1)}, f32[64,1,16,128]{3,0,2,1:T(8,128)S(1)}, u32[]{:S(2)}, u32[]{:S(2)}) collective-permute-start(f32[64,1,16,128]{3,0,2,1:T(8,128)S(1)} %get-tuple-element.119), channel_id=1, source_target_pairs={{0,8},{8,16},{16,24},{24,32},{32,40},{40,48},{48,56},{56,64},{64,7... | collective-permute-start | bytes 1572872 | tf_op jit(solution)/shard_map/ppermute | solution.py:16
  221.6 12.5 %collective-permute-start.25 = (f32[64,1,16,128]{3,0,2,1:T(8,128)S(1)}, f32[64,1,16,128]{3,0,2,1:T(8,128)S(1)}, u32[]{:S(2)}, u32[]{:S(2)}) collective-permute-start(f32[64,1,16,128]{3,0,2,1:T(8,128)S(1)} %get-tuple-element.120), channel_id=1, source_target_pairs={{8,0},{16,8},{24,16},{32,24},{40,32},{48,40},{56,48},{64,56},{72,6... | collective-permute-start | bytes 1572872 | tf_op jit(solution)/shard_map/ppermute | solution.py:17
  234.2 7.4 %collective-permute-start.26 = (f32[64,10,1,128]{3,0,2,1:T(8,128)S(1)}, f32[64,10,1,128]{3,0,2,1:T(8,128)S(1)}, u32[]{:S(2)}, u32[]{:S(2)}) collective-permute-start(f32[64,10,1,128]{3,0,2,1:T(8,128)S(1)} %get-tuple-element.107), channel_id=1, source_target_pairs={{0,1},{1,2},{2,3},{3,4},{4,5},{5,6},{6,7},{8,9},{9,10},{10,11},{11... | collective-permute-start | bytes 983048 | tf_op jit(solution)/shard_map/ppermute | solution.py:16
  240.1 7.1 %collective-permute-start.27 = (f32[64,10,1,128]{3,0,2,1:T(8,128)S(1)}, f32[64,10,1,128]{3,0,2,1:T(8,128)S(1)}, u32[]{:S(2)}, u32[]{:S(2)}) collective-permute-start(f32[64,10,1,128]{3,0,2,1:T(8,128)S(1)} %get-tuple-element.108), channel_id=1, source_target_pairs={{1,0},{2,1},{3,2},{4,3},{5,4},{6,5},{7,6},{9,8},{10,9},{11,10},{12... | collective-permute-start | bytes 983048 | tf_op jit(solution)/shard_map/ppermute | solution.py:17
  (12 other events, 243.1 us)
